TPU v7x, 32 devices: a whole 2x2x4 slice. The times are simulated.
32 devices in a mesh: gz: 4 (over y, core), xy: 8 (over z, x).
Axes of the slice: x: 2, y: 2, z: 4, core: 2. Of those that a mesh axis runs over, the one named last changes fastest.
Arguments:
- cotangent: bfloat16 [4, 8, 9, 128, 128], P('gz', 'xy'), may hold values from -6 to 6
- displacement: float32 [4, 8, 3, 32, 128], P('gz', 'xy'), may hold values from -2 to 2
- neighbours: int32 [4, 8, 32, 128], P('gz', 'xy'), may hold values from 0 to 2303
- counts: int32 [4, 8, 128], P('gz', 'xy'), may hold values from 8 to 32, as said below
- atom_feat: bfloat16 [4, 8, 256, 128], P('gz', 'xy'), may hold values from -6 to 6
- radial_weight: float32 [3, 16, 128], replicated, may hold values from -1.5 to 1.5
- mix_weight: bfloat16 [3, 128, 128], replicated, may hold values from -0.5 to 0.5
Outputs:
- atom_grad: float32 [4, 8, 256, 128], P('gz', 'xy')
- radial_grad: float32 [3, 16, 128], replicated
- mix_grad: float32 [3, 128, 128], replicated
Inputs may be any that keep to these rules, and one draw needn't show every extreme that they name: `counts`: the first probe of the first brick uses all 32 slots and the first probe of the second brick uses 32 // 4.
All inputs are finite; a program needn't handle non-finite values.
Results may differ from a plain program's by a relative error of at most 0.0051.
Values may be sent and summed in bfloat16 or wider, within the bound.
A program may use at most 64 MiB of HBM per device.

v0:
```python
import math
import jax
import jax.numpy as jnp
from jax import lax
from jax.sharding import PartitionSpec as P

CUTOFF = 4.0
LEVEL_SPANS = ((0, 1), (1, 4), (4, 9))


def padded(cells, sides, width):
    for axis, dim in sides:
        count = lax.axis_size(axis)
        head = lax.slice_in_dim(cells, 0, width, axis=dim)
        tail = lax.slice_in_dim(cells, cells.shape[dim] - width, cells.shape[dim], axis=dim)
        cells = jnp.concatenate(
            [
                lax.ppermute(tail, axis, [(i, (i + 1) % count) for i in range(count)]),
                cells,
                lax.ppermute(head, axis, [((i + 1) % count, i) for i in range(count)]),
            ],
            axis=dim,
        )
    return cells


def harmonics(disp):
    scaled = disp / CUTOFF
    coord_x, coord_y, coord_z = (scaled[0], scaled[1], scaled[2])
    root3, root5, root15 = (math.sqrt(3.0), math.sqrt(5.0), math.sqrt(15.0))
    return jnp.stack(
        [
            jnp.ones_like(coord_x),
            root3 * coord_x,
            root3 * coord_y,
            root3 * coord_z,
            root15 * coord_x * coord_y,
            root15 * coord_y * coord_z,
            0.5 * root5 * (2.0 * coord_z * coord_z - coord_x * coord_x - coord_y * coord_y),
            root15 * coord_x * coord_z,
            0.5 * root15 * (coord_x * coord_x - coord_y * coord_y),
        ]
    )


def basis(disp, nbasis):
    distance = jnp.sqrt(jnp.sum(disp * disp, axis=0))
    centres = jnp.arange(nbasis).astype(jnp.float32) * (CUTOFF / (nbasis - 1))
    sharpness = ((nbasis - 1) / CUTOFF) ** 2
    envelope = 0.5 * (jnp.cos(math.pi * distance / CUTOFF) + 1.0)
    shaped = centres.reshape((nbasis,) + (1,) * distance.ndim)
    return jnp.exp(-sharpness * (distance[None] - shaped) ** 2) * envelope[None]


def exact(form, left, right):
    return jnp.einsum(form, left, right, precision=lax.Precision.HIGHEST)


def matmul(form, left, right):
    return jnp.einsum(form, left, right, preferred_element_type=jnp.float32)


def gate_backward(moments, mix_weight, cotangent):
    mixed_out = [
        matmul("mpc,cd->mpd", moments[span_start:span_end], mix_weight[level])
        for level, (span_start, span_end) in enumerate(LEVEL_SPANS)
    ]
    scalar = mixed_out[0][0]
    gating = jax.nn.sigmoid(scalar)
    gate_slope = gating * (1.0 - gating)
    cot_float = cotangent.astype(jnp.float32)
    higher = jnp.concatenate(mixed_out[1:], 0)
    first_term = (
        cot_float[0] * (gating + scalar * gate_slope)
        + jnp.sum(cot_float[1:] * higher, 0) * gate_slope
    )
    dmixed = jnp.concatenate([first_term[None], cot_float[1:] * gating[None]], 0).astype(
        jnp.bfloat16
    )
    dmoments = jnp.concatenate(
        [
            matmul("mpd,cd->mpc", dmixed[span_start:span_end], mix_weight[level])
            for level, (span_start, span_end) in enumerate(LEVEL_SPANS)
        ],
        0,
    ).astype(jnp.bfloat16)
    mix_part = jnp.stack(
        [
            matmul("mpc,mpd->cd", moments[span_start:span_end], dmixed[span_start:span_end])
            for span_start, span_end in LEVEL_SPANS
        ]
    )
    return (dmoments, mix_part)


def shards(cotangent, displacement, neighbours, counts, atom_feat, radial_weight, mix_weight):
    cot_local = cotangent[0, 0]
    disp_local = displacement[0, 0]
    neighbour_local_index = neighbours[0, 0]
    probe_tally = counts[0, 0]
    slot_count = neighbour_local_index.shape[0]
    probe_count = neighbour_local_index.shape[1]
    natom = atom_feat.shape[2]
    channels = atom_feat.shape[3]
    nbasis = radial_weight.shape[1]
    filled_slots = (
        lax.broadcasted_iota(jnp.int32, (slot_count, probe_count), 0) < probe_tally[None]
    ).astype(jnp.float32)
    angular = harmonics(disp_local) * filled_slots[None]
    radial_basis = basis(disp_local, nbasis)
    atom_table = padded(atom_feat, (("gz", 0), ("xy", 1)), 1).reshape(9 * natom, channels)
    features = atom_table[neighbour_local_index].astype(jnp.float32)
    radial = exact("bkp,lbc->lkpc", radial_basis, radial_weight)
    pieces = []
    for level, (span_start, span_end) in enumerate(LEVEL_SPANS):
        weighted = radial[level] * features
        pieces.append(jnp.sum(angular[span_start:span_end, :, :, None] * weighted[None], axis=1))
    moments = jnp.concatenate(pieces, 0).astype(jnp.bfloat16)
    dmoments, mix_part = gate_backward(moments, mix_weight, cot_local)
    mix_total = lax.psum(mix_part, ("gz", "xy"))
    dmoment_float = dmoments.astype(jnp.float32)
    contrib = jnp.zeros(features.shape, jnp.float32)
    radial_parts = []
    for level, (span_start, span_end) in enumerate(LEVEL_SPANS):
        traced = jnp.sum(
            angular[span_start:span_end, :, :, None] * dmoment_float[span_start:span_end, None],
            axis=0,
        )
        contrib = contrib + radial[level] * traced
        radial_parts.append(exact("bkp,kpc->bc", radial_basis, features * traced))
    grads = (
        jnp.zeros((9 * natom, channels), jnp.float32)
        .at[neighbour_local_index.reshape(-1)]
        .add(contrib.reshape(-1, channels))
    )
    radial_part = jnp.stack(radial_parts)
    radial_total = lax.psum(radial_part, ("gz", "xy"))
    blocks = grads.reshape(3, 3, natom, channels)
    outer_rows = jnp.stack([blocks[0], blocks[2]], 0)
    arrived = padded(outer_rows, (("gz", 0),), 1)
    columns = blocks[1] + arrived[0] + arrived[3]
    outer_columns = jnp.stack([columns[0], columns[2]], 0)
    landed = padded(outer_columns, (("xy", 0),), 1)
    owned = columns[1] + landed[0] + landed[3]
    return (owned[None, None], radial_total, mix_total)


def solution(mesh):
    in_specs = (
        P("gz", "xy", None, None, None),
        P("gz", "xy", None, None, None),
        P("gz", "xy", None, None),
        P("gz", "xy", None),
        P("gz", "xy", None, None),
        P(),
        P(),
    )
    out_specs = (P("gz", "xy", None, None), P(), P())
    return jax.shard_map(shards, mesh=mesh, in_specs=in_specs, out_specs=out_specs, check_vma=False)
```

profile of v0, /device:TPU:10, one launch (start us, length us, event | category | flops | bytes accessed | tf_op | source)
XLA Modules:
  0.0 237.2 jit_solution(9430039311791269466)
XLA Ops:
  7.3 1.7 collective-permute-start.1
  9.0 0.8 multiply_reduce_fusion.5
  10.7 1.3 compare_select_fusion
  12.1 7.2 %convolution_bitcast_fusion = f32[3,32,128,128]{3,2,0,1:T(8,128)} fusion(f32[32,128]{1,0:T(8,128)S(1)} %get-tuple-element.23, f32[16]{0:T(128)S(1)} %convert_multiply_fusion, f32[32,128]{1,0:T(8,128)S(1)} %get-tuple-element.22, f32[3,16,128]{2,1,0:T(8,128)S(1)} %copy-done), kind=kOutput, calls=%fused_computation.6 | convolution fusion | flops 302252032 | bytes 6348864 | tf_op jit(solution)/shard_map/bkp,lbc->lkpc/dot_general | solution.py:56
  19.4 0.9 convert_element_type.43
  20.3 1.6 collective-permute-start.2
  22.4 8.9 %collective-permute-done.2 = bf16[3,1,256,128]{3,2,1,0:T(8,128)(2,1)S(1)} collective-permute-done((bf16[3,1,256,128]{3,2,1,0:T(8,128)(2,1)S(1)}, bf16[3,1,256,128]{3,2,1,0:T(8,128)(2,1)S(1)}, u32[]{:S(2)}, u32[]{:S(2)}) %collective-permute-start.2) | collective-permute-done | bytes 196640 | tf_op jit(solution)/shard_map/ppermute | solution.py:18
  31.4 12.1 %gather_fusion = bf16[4096,128]{1,0:T(8,128)(2,1)S(1)} fusion(bf16[2304,128]{1,0:T(8,128)(2,1)S(1)} %bitcast.167, s32[4096]{0:T(1024)S(1)} %fusion.74), kind=kCustom, calls=%fused_computation | custom fusion | bytes 2113536 | tf_op jit(solution)/shard_map/gather | solution.py:112
  43.7 3.6 %fusion.83 = (f32[1,32,128,128]{3,2,0,1:T(8,128)S(1)}, bf16[128,128]{1,0:T(8,128)(2,1)S(1)}, f32[32,128,128]{2,1,0:T(8,128)S(1)}, f32[32,128,128]{2,1,0:T(8,128)...) fusion(f32[3,32,128,128]{3,2,0,1:T(8,128)} %convolution_bitcast_fusion, ...), kind=kLoop, calls=%fused_computation.141 | loop fusion | flops 3129344 | bytes 19972096 | tf_op jit(solution)/shard_map/slice | solution.py:129
  47.3 2.0 multiply_reduce_fusion.3
  49.4 3.1 %multiply_reduce_fusion.1 = bf16[5,128,128]{2,1,0:T(8,128)(2,1)S(1)} fusion(f32[32,128,128]{2,1,0:T(8,128)S(1)} %get-tuple-element.7, f32[5,32,128]{2,1,0:T(8,128)S(1)} %slice.162), kind=kLoop, calls=%fused_computation.3 | loop fusion | flops 5160960 | bytes 2342912 | tf_op jit(solution)/shard_map/reduce_sum | solution.py:117
  54.1 2.1 multiply_reduce_fusion.2
  56.3 2.1 fusion.11
  58.4 2.0 fusion.14
  60.4 3.2 %multiply_reduce_fusion = f32[32,128,128]{2,1,0:T(8,128)S(1)} fusion(f32[5,128,128]{2,1,0:T(8,128)S(1)} %fusion.27, f32[5,32,128]{2,1,0:T(8,128)S(1)} %slice.162), kind=kLoop, calls=%fused_computation.2 | loop fusion | flops 4718592 | bytes 2506752 | tf_op jit(solution)/shard_map/reduce_sum | solution.py:125
  63.6 2.4 %fusion = f32[4096,128]{1,0:T(8,128)} fusion(f32[32,128,128]{2,1,0:T(8,128)S(1)} %multiply_reduce_fusion, f32[1,32,128,128]{3,2,0,1:T(8,128)S(1)} %get-tuple-element.9, f32[32,128,128]{2,1,0:T(8,128)S(1)} %multiply_reduce_fusion.2, f32[1,32,128,128]{3,2,0,1:T(8,128)S(1)} %get-tuple-element.10, f32[1,32,128,128]{3,2,0,1:T(8,128)S(1)} %get-tuple-element.5, ...), kind=kLoop, calls=%fused_computation.8 | loop fusion | flops 3145728 | bytes 12664832 | tf_op jit(solution)/shard_map/add | solution.py:129
  66.1 22.9 %scatter_custom_fusion = f32[2304,128]{1,0:T(8,128)S(1)} fusion(s32[4096]{0:T(1024)} %bitcast.176, f32[4096,128]{1,0:T(8,128)} %fusion, f32[]{:T(128)} %constant.14.clone.1), kind=kCustom, calls=%fused_computation.36 | custom fusion | flops 524288 | bytes 1180160 | tf_op jit(solution)/shard_map/scatter-add | solution.py:134
  89.2 1.7 collective-permute-start.5
  91.1 1.3 fusion.17
  92.5 7.3 %collective-permute-done.4 = f32[1,3,256,128]{3,2,1,0:T(8,128)S(1)} collective-permute-done((f32[1,3,256,128]{3,2,1,0:T(8,128)S(1)}, f32[1,3,256,128]{3,2,1,0:T(8,128)S(1)}, u32[]{:S(2)}, u32[]{:S(2)}) %collective-permute-start.4) | collective-permute-done | bytes 393248 | tf_op jit(solution)/shard_map/ppermute | solution.py:18
  99.9 2.5 %collective-permute-start.6 = (f32[1,256,128]{2,1,0:T(8,128)S(1)}, f32[1,256,128]{2,1,0:T(8,128)S(1)}, u32[]{:S(2)}, u32[]{:S(2)}) collective-permute-start(f32[1,256,128]{2,1,0:T(8,128)S(1)} %get-tuple-element.16), channel_id=1, source_target_pairs={{0,1},{1,2},{2,3},{3,4},{4,5},{5,6},{6,7},{7,0},{8,9},{9,10},{10,1... | collective-permute-start | bytes 393224 | tf_op jit(solution)/shard_map/ppermute | solution.py:18
  103.1 43.0 %psum.14 = f32[3,16,128]{2,1,0:T(8,128)} all-reduce(f32[3,16,128]{2,1,0:T(8,128)S(1)} %pad_maximum_fusion.4), channel_id=1, replica_groups=mesh['gz'=4,'xy'=8] {'gz','xy'}, use_global_device_ids=true, to_apply=%region_8.0 | all-reduce | flops 6144 | bytes 49152 | tf_op jit(solution)/shard_map/psum | solution.py:137
  146.8 81.9 %all-reduce.2.cloned.1.call-done = f32[3,128,128]{2,1,0:T(8,128)} async-done(((f32[3,128,128]{2,1,0:T(8,128)}), f32[3,128,128]{2,1,0:T(8,128)}) %all-reduce.2.cloned.1.call-update) | async-done | bytes 196624 | tf_op jit(solution)/shard_map/psum | solution.py:120
  228.7 1.6 copy.28
  (80 shorter events, 5.2 us)
Async XLA Ops:
  7.2 4.9 %copy-start = (f32[3,16,128]{2,1,0:T(8,128)S(1)}, f32[3,16,128]{2,1,0:T(8,128)}, u32[]{:S(2)}) copy-start(f32[3,16,128]{2,1,0:T(8,128)} %param.12) | copy-start | bytes 73732
  7.2 221.5 %all-reduce.2.cloned.1.call-start = ((), (), s32[]{:S(2)}) async-start(), calls=%async_computation | async-start | bytes 393216 | tf_op jit(solution)/shard_map/psum | solution.py:120
  7.2 13.0 %collective-permute-start = (bf16[1,1,256,128]{3,2,1,0:T(8,128)(2,1)}, bf16[1,1,256,128]{3,2,1,0:T(8,128)(2,1)S(1)}, u32[]{:S(2)}, u32[]{:S(2)}) collective-permute-start(bf16[1,1,256,128]{3,2,1,0:T(8,128)(2,1)} %param.11), channel_id=1, source_target_pairs={{0,8},{8,16},{16,24},{24,0},{1,9},{9,17},{17,25},{25,1},{2,10},{10... | collective-permute-start | bytes 196616 | tf_op jit(solution)/shard_map/ppermute | solution.py:18
  7.3 13.0 %collective-permute-start.1 = (bf16[1,1,256,128]{3,2,1,0:T(8,128)(2,1)}, bf16[1,1,256,128]{3,2,1,0:T(8,128)(2,1)S(1)}, u32[]{:S(2)}, u32[]{:S(2)}) collective-permute-start(bf16[1,1,256,128]{3,2,1,0:T(8,128)(2,1)} %param.11), channel_id=1, source_target_pairs={{8,0},{16,8},{24,16},{0,24},{9,1},{17,9},{25,17},{1,25},{10,2},{18... | collective-permute-start | bytes 196616 | tf_op jit(solution)/shard_map/ppermute | solution.py:20
  9.0 47.2 %copy-start.11 = (f32[16]{0:T(128)}, f32[16]{0:T(128)S(1)}, u32[]{:S(2)}) copy-start(f32[16]{0:T(128)S(1)} %convert_multiply_fusion) | copy-start | bytes 196
  12.1 7.3 %copy-start.4 = (bf16[1,1,9,128,128]{4,3,2,1,0:T(8,128)(2,1)S(1)}, bf16[1,1,9,128,128]{4,3,2,1,0:T(8,128)(2,1)}, u32[]{:S(2)}) copy-start(bf16[1,1,9,128,128]{4,3,2,1,0:T(8,128)(2,1)} %param.7) | copy-start | bytes 884740
  12.1 8.2 %copy-start.6 = (bf16[1,1,256,128]{3,2,1,0:T(8,128)(2,1)S(1)}, bf16[1,1,256,128]{3,2,1,0:T(8,128)(2,1)}, u32[]{:S(2)}) copy-start(bf16[1,1,256,128]{3,2,1,0:T(8,128)(2,1)} %param.11) | copy-start | bytes 196612
  12.1 10.3 %copy-start.7 = (s32[1,1,32,128]{3,2,1,0:T(8,128)S(1)}, s32[1,1,32,128]{3,2,1,0:T(8,128)}, u32[]{:S(2)}) copy-start(s32[1,1,32,128]{3,2,1,0:T(8,128)} %param.9) | copy-start | bytes 49156
  19.3 24.3 %copy-start.8 = (f32[32,128]{1,0:T(8,128)}, f32[32,128]{1,0:T(8,128)S(1)}, u32[]{:S(2)}) copy-start(f32[32,128]{1,0:T(8,128)S(1)} %get-tuple-element.19) | copy-start | bytes 49156
  20.3 11.0 %collective-permute-start.2 = (bf16[3,1,256,128]{3,2,1,0:T(8,128)(2,1)S(1)}, bf16[3,1,256,128]{3,2,1,0:T(8,128)(2,1)S(1)}, u32[]{:S(2)}, u32[]{:S(2)}) collective-permute-start(bf16[3,1,256,128]{3,2,1,0:T(8,128)(2,1)S(1)} %constant_dynamic-update-slice_fusion.9), channel_id=1, source_target_pairs={{0,1},{1,2},{2,3},{3,4},{4,5},{5,6},{6,7},{7,0},{8,9},{9,10},{10,1... | collective-permute-start | bytes 589832 | tf_op jit(solution)/shard_map/ppermute | solution.py:18
  21.9 9.4 %collective-permute-start.3 = (bf16[3,1,256,128]{3,2,1,0:T(8,128)(2,1)S(1)}, bf16[3,1,256,128]{3,2,1,0:T(8,128)(2,1)S(1)}, u32[]{:S(2)}, u32[]{:S(2)}) collective-permute-start(bf16[3,1,256,128]{3,2,1,0:T(8,128)(2,1)S(1)} %constant_dynamic-update-slice_fusion.9), channel_id=1, source_target_pairs={{1,0},{2,1},{3,2},{4,3},{5,4},{6,5},{7,6},{0,7},{9,8},{10,9},{11,1... | collective-permute-start | bytes 589832 | tf_op jit(solution)/shard_map/ppermute | solution.py:20
  47.3 2.0 copy-start.5
  49.3 3.6 %copy-start.3 = (f32[1,1,9,128,128]{4,3,2,1,0:T(8,128)S(1)}, f32[1,1,9,128,128]{4,3,2,1,0:T(8,128)}, u32[]{:S(2)}) copy-start(f32[1,1,9,128,128]{4,3,2,1,0:T(8,128)} %convert_element_type.43) | copy-start | bytes 1769476
  53.9 2.4 %copy-start.9 = (f32[32,128]{1,0:T(8,128)S(1)}, f32[32,128]{1,0:T(8,128)}, u32[]{:S(2)}) copy-start(f32[32,128]{1,0:T(8,128)} %copy-done.8) | copy-start | bytes 49156
  63.6 2.4 %copy-start.1 = (f32[32,128,128]{2,1,0:T(8,128)}, f32[32,128,128]{2,1,0:T(8,128)S(1)}, u32[]{:S(2)}) copy-start(f32[32,128,128]{2,1,0:T(8,128)S(1)} %multiply_reduce_fusion) | copy-start | bytes 6291460
  66.1 25.0 %copy-start.12 = (f32[16]{0:T(128)S(1)}, f32[16]{0:T(128)}, u32[]{:S(2)}) copy-start(f32[16]{0:T(128)} %copy-done.11) | copy-start | bytes 196
  89.0 2.1 copy-start.2
  89.1 10.7 %collective-permute-start.4 = (f32[1,3,256,128]{3,2,1,0:T(8,128)S(1)}, f32[1,3,256,128]{3,2,1,0:T(8,128)S(1)}, u32[]{:S(2)}, u32[]{:S(2)}) collective-permute-start(f32[1,3,256,128]{3,2,1,0:T(8,128)S(1)} %bitcast.174), channel_id=1, source_target_pairs={{0,8},{8,16},{16,24},{24,0},{1,9},{9,17},{17,25},{25,1},{2,10},{10... | collective-permute-start | bytes 1179656 | tf_op jit(solution)/shard_map/ppermute | solution.py:18
  89.2 10.6 %collective-permute-start.5 = (f32[1,3,256,128]{3,2,1,0:T(8,128)S(1)}, f32[1,3,256,128]{3,2,1,0:T(8,128)S(1)}, u32[]{:S(2)}, u32[]{:S(2)}) collective-permute-start(f32[1,3,256,128]{3,2,1,0:T(8,128)S(1)} %bitcast.173), channel_id=1, source_target_pairs={{8,0},{16,8},{24,16},{0,24},{9,1},{17,9},{25,17},{1,25},{10,2},{18... | collective-permute-start | bytes 1179656 | tf_op jit(solution)/shard_map/ppermute | solution.py:20
  92.5 10.6 %copy-start.10 = (f32[1,16,128]{2,1,0:T(8,128)S(1)}, f32[1,16,128]{2,1,0:T(8,128)}, u32[]{:S(2)}) copy-start(f32[1,16,128]{2,1,0:T(8,128)} %fusion.11) | copy-start | bytes 24580
  99.9 46.2 %collective-permute-start.6 = (f32[1,256,128]{2,1,0:T(8,128)S(1)}, f32[1,256,128]{2,1,0:T(8,128)S(1)}, u32[]{:S(2)}, u32[]{:S(2)}) collective-permute-start(f32[1,256,128]{2,1,0:T(8,128)S(1)} %get-tuple-element.16), channel_id=1, source_target_pairs={{0,1},{1,2},{2,3},{3,4},{4,5},{5,6},{6,7},{7,0},{8,9},{9,10},{10,1... | collective-permute-start | bytes 393224 | tf_op jit(solution)/shard_map/ppermute | solution.py:18
  102.4 43.7 %collective-permute-start.7 = (f32[1,256,128]{2,1,0:T(8,128)S(1)}, f32[1,256,128]{2,1,0:T(8,128)S(1)}, u32[]{:S(2)}, u32[]{:S(2)}) collective-permute-start(f32[1,256,128]{2,1,0:T(8,128)S(1)} %get-tuple-element.17), channel_id=1, source_target_pairs={{1,0},{2,1},{3,2},{4,3},{5,4},{6,5},{7,6},{0,7},{9,8},{10,9},{11,1... | collective-permute-start | bytes 393224 | tf_op jit(solution)/shard_map/ppermute | solution.py:20
Sparse Core Ops, SparseCore 0:
  103.2 125.4 all-reduce.1
where the time goes:
time: 238 us; the launch traced here: 237 us
  waiting for transfers between devices  98.2 us (41%)
  other arithmetic  45.1 us (19%)
  blocking collectives  43 us (18%)
  between operations  14.5 us (6%)
  matrix products  14.3 us (6%)
  local copies, waits for them, and re-layouts  14 us (6%)
  starting transfers between devices  8.19 us (3%)
    psum x1, waiting for transfers between devices, shards(): mix_total = lax.psum(mix_part, ('gz', 'xy'))  81.9 us
    psum x1, blocking collectives, shards(): radial_total = lax.psum(radial_part, ('gz', 'xy'))  43 us
    scatter-add x1, other arithmetic, shards(): grads = jnp.zeros((9 * natom, channels), jnp.float32).at[neighbour_local_...  22.9 us
    ppermute x4, waiting for transfers between devices, padded(): lax.ppermute(tail, axis, [(i, (i + 1) % count) for i in range(count)])  16.2 us
    dot_general x4, matrix products, exact(): return jnp.einsum(form, left, right, precision=lax.Precision.HIGHEST)  12.7 us
    gather x1, local copies, waits for them, and re-layouts, shards(): features = atom_table[neighbour_local_index].astype(jnp.float32)  12.1 us
    reduce_sum x2, other arithmetic, shards(): jnp.sum(angular[span_start:span_end, :, :, None] * dmoment_float[span_sta...  5.34 us
    reduce_sum x2, other arithmetic, shards(): jnp.sum(angular[span_start:span_end, :, :, None] * weighted[None], axis=1)  5.1 us
  transfers between devices with their start and end apart: 9, of which 3 were waited for; matrix products, arithmetic and copies ran while one was open for 6% of the time, Pallas kernels for 0%

commit v1 on v0

--- a/solution.py
+++ b/solution.py
@@ -3,6 +3,7 @@
 import jax.numpy as jnp
 from jax import lax
 from jax.sharding import PartitionSpec as P
+from jax.lax import psum
 
 CUTOFF = 4.0
 LEVEL_SPANS = ((0, 1), (1, 4), (4, 9))
@@ -117,7 +118,7 @@
         pieces.append(jnp.sum(angular[span_start:span_end, :, :, None] * weighted[None], axis=1))
     moments = jnp.concatenate(pieces, 0).astype(jnp.bfloat16)
     dmoments, mix_part = gate_backward(moments, mix_weight, cot_local)
-    mix_total = lax.psum(mix_part, ("gz", "xy"))
+    mix_total = psum(psum(mix_part, axis_name="xy"), axis_name="gz")
     dmoment_float = dmoments.astype(jnp.float32)
     contrib = jnp.zeros(features.shape, jnp.float32)
     radial_parts = []

time: 238 us -> 187 us (0.79)
  waiting for transfers between devices: 98.2 us -> 44.6 us
  other arithmetic: 45.1 us -> 47.9 us
    psum x1 -> x2, waiting for transfers between devices: 81.9 us -> 29.7 us  [shards(): mix_total = psum(psum(mix_part, axis_name='xy'), axis_name='gz')]
  transfers between devices with their start and end apart: 9 -> 10, of which waited for: 3 -> 3; matrix products, arithmetic and copies ran while one was open for 6% -> 26% of each run, Pallas kernels for 0% -> 0%
where the time goes in v1:
time: 187 us; the launch traced here: 185 us
  other arithmetic  47.9 us (26%)
  waiting for transfers between devices  44.6 us (24%)
  blocking collectives  43 us (23%)
  between operations  14.5 us (8%)
  local copies, waits for them, and re-layouts  14.2 us (8%)
  matrix products  13 us (7%)
  starting transfers between devices  8.21 us (4%)
    psum x1, blocking collectives, shards(): radial_total = lax.psum(radial_part, ('gz', 'xy'))  43 us
    psum x2, waiting for transfers between devices, shards(): mix_total = psum(psum(mix_part, axis_name='xy'), axis_name='gz')  29.7 us
    scatter-add x1, other arithmetic, shards(): grads = jnp.zeros((9 * natom, channels), jnp.float32).at[neighbour_local_...  22.9 us
    ppermute x4, waiting for transfers between devices, padded(): lax.ppermute(tail, axis, [(i, (i + 1) % count) for i in range(count)])  14.8 us
    gather x1, local copies, waits for them, and re-layouts, shards(): features = atom_table[neighbour_local_index].astype(jnp.float32)  12.1 us
    dot_general x4, matrix products, exact(): return jnp.einsum(form, left, right, precision=lax.Precision.HIGHEST)  11.3 us
    reduce_sum x2, other arithmetic, shards(): jnp.sum(angular[span_start:span_end, :, :, None] * dmoment_float[span_sta...  5.33 us
    reduce_sum x2, other arithmetic, shards(): jnp.sum(angular[span_start:span_end, :, :, None] * weighted[None], axis=1)  5.1 us
  transfers between devices with their start and end apart: 10, of which 3 were waited for; matrix products, arithmetic and copies ran while one was open for 26% of the time, Pallas kernels for 0%

profile of v1, /device:TPU:10, one launch (start us, length us, event | category | flops | bytes accessed | tf_op | source)
XLA Modules:
  0.0 185.4 jit_solution(9806665214811575056)
XLA Ops:
  7.3 1.7 collective-permute-start.1
  9.0 0.8 multiply_reduce_fusion.5
  10.7 1.3 compare_select_fusion
  12.1 7.2 %convolution_bitcast_fusion = f32[3,32,128,128]{3,2,0,1:T(8,128)} fusion(f32[32,128]{1,0:T(8,128)S(1)} %get-tuple-element.23, f32[16]{0:T(128)S(1)} %convert_multiply_fusion, f32[32,128]{1,0:T(8,128)S(1)} %get-tuple-element.22, f32[3,16,128]{2,1,0:T(8,128)S(1)} %copy-done), kind=kOutput, calls=%fused_computation.6 | convolution fusion | flops 302252032 | bytes 6348864 | tf_op jit(solution)/shard_map/bkp,lbc->lkpc/dot_general | solution.py:57
  19.4 0.9 convert_element_type.43
  20.3 1.6 collective-permute-start.2
  22.4 8.9 %collective-permute-done.2 = bf16[3,1,256,128]{3,2,1,0:T(8,128)(2,1)S(1)} collective-permute-done((bf16[3,1,256,128]{3,2,1,0:T(8,128)(2,1)S(1)}, bf16[3,1,256,128]{3,2,1,0:T(8,128)(2,1)S(1)}, u32[]{:S(2)}, u32[]{:S(2)}) %collective-permute-start.2) | collective-permute-done | bytes 196640 | tf_op jit(solution)/shard_map/ppermute | solution.py:19
  31.4 12.1 %gather_fusion = bf16[4096,128]{1,0:T(8,128)(2,1)S(1)} fusion(bf16[2304,128]{1,0:T(8,128)(2,1)S(1)} %bitcast.167, s32[4096]{0:T(1024)S(1)} %fusion.74), kind=kCustom, calls=%fused_computation | custom fusion | bytes 2113536 | tf_op jit(solution)/shard_map/gather | solution.py:113
  43.6 5.1 %fusion.83 = (f32[1,32,128,128]{3,2,0,1:T(8,128)}, bf16[128,128]{1,0:T(8,128)(2,1)S(1)}, f32[32,128,128]{2,1,0:T(8,128)S(1)}, f32[32,128,128]{2,1,0:T(8,128)S(1)...) fusion(f32[3,32,128,128]{3,2,0,1:T(8,128)} %convolution_bitcast_fusion, ...), kind=kLoop, calls=%fused_computation.141 | loop fusion | flops 3129344 | bytes 19972096 | tf_op jit(solution)/shard_map/slice | solution.py:130
  48.7 2.0 %multiply_reduce_fusion.3 = bf16[3,128,128]{2,1,0:T(8,128)(2,1)S(1)} fusion(f32[32,128,128]{2,1,0:T(8,128)S(1)} %get-tuple-element.8, f32[3,32,128]{2,1,0:T(8,128)S(1)} %slice.160), kind=kLoop, calls=%fused_computation.5 | loop fusion | flops 3096576 | bytes 2244608 | tf_op jit(solution)/shard_map/reduce_sum | solution.py:118
  50.9 3.1 %multiply_reduce_fusion.1 = bf16[5,128,128]{2,1,0:T(8,128)(2,1)S(1)} fusion(f32[32,128,128]{2,1,0:T(8,128)S(1)} %get-tuple-element.7, f32[5,32,128]{2,1,0:T(8,128)S(1)} %slice.162), kind=kLoop, calls=%fused_computation.3 | loop fusion | flops 5160960 | bytes 2342912 | tf_op jit(solution)/shard_map/reduce_sum | solution.py:118
  56.6 2.1 %multiply_reduce_fusion.2 = f32[32,128,128]{2,1,0:T(8,128)S(1)} fusion(f32[3,128,128]{2,1,0:T(8,128)S(1)} %maximum_convert_fusion, f32[3,32,128]{2,1,0:T(8,128)S(1)} %slice.160), kind=kLoop, calls=%fused_computation.4 | loop fusion | flops 2621440 | bytes 2342912 | tf_op jit(solution)/shard_map/reduce_sum | solution.py:126
  58.7 3.2 %multiply_reduce_fusion = f32[32,128,128]{2,1,0:T(8,128)S(1)} fusion(f32[5,128,128]{2,1,0:T(8,128)S(1)} %fusion.27, f32[5,32,128]{2,1,0:T(8,128)S(1)} %slice.162), kind=kLoop, calls=%fused_computation.2 | loop fusion | flops 4718592 | bytes 2506752 | tf_op jit(solution)/shard_map/reduce_sum | solution.py:126
  62.0 3.7 %fusion = f32[4096,128]{1,0:T(8,128)} fusion(f32[32,128,128]{2,1,0:T(8,128)S(1)} %multiply_reduce_fusion, f32[1,32,128,128]{3,2,0,1:T(8,128)S(1)} %copy-done.6, f32[32,128,128]{2,1,0:T(8,128)S(1)} %multiply_reduce_fusion.2, f32[1,32,128,128]{3,2,0,1:T(8,128)} %get-tuple-element.10, f32[1,32,128,128]{3,2,0,1:T(8,128)S(1)} %copy-done.5, ...), kind=kLoop, calls=%fused_computation.8 | loop fusion | flops 3145728 | bytes 12664832 | tf_op jit(solution)/shard_map/add | solution.py:130
  65.7 22.9 %scatter_custom_fusion = f32[2304,128]{1,0:T(8,128)S(1)} fusion(s32[4096]{0:T(1024)} %bitcast.176, f32[4096,128]{1,0:T(8,128)} %fusion, f32[]{:T(128)} %constant.14.clone.1), kind=kCustom, calls=%fused_computation.36 | custom fusion | flops 524288 | bytes 1180160 | tf_op jit(solution)/shard_map/scatter-add | solution.py:135
  88.8 1.7 collective-permute-start.5
  90.6 1.3 fusion.14
  92.2 1.3 fusion.17
  93.5 6.0 %collective-permute-done.4 = f32[1,3,256,128]{3,2,1,0:T(8,128)S(1)} collective-permute-done((f32[1,3,256,128]{3,2,1,0:T(8,128)S(1)}, f32[1,3,256,128]{3,2,1,0:T(8,128)S(1)}, u32[]{:S(2)}, u32[]{:S(2)}) %collective-permute-start.4) | collective-permute-done | bytes 393248 | tf_op jit(solution)/shard_map/ppermute | solution.py:19
  99.6 2.5 %collective-permute-start.6 = (f32[1,256,128]{2,1,0:T(8,128)S(1)}, f32[1,256,128]{2,1,0:T(8,128)S(1)}, u32[]{:S(2)}, u32[]{:S(2)}) collective-permute-start(f32[1,256,128]{2,1,0:T(8,128)S(1)} %get-tuple-element.16), channel_id=1, source_target_pairs={{0,1},{1,2},{2,3},{3,4},{4,5},{5,6},{6,7},{7,0},{8,9},{9,10},{10,1... | collective-permute-start | bytes 393224 | tf_op jit(solution)/shard_map/ppermute | solution.py:19
  102.0 1.4 fusion.11
  103.5 43.0 %psum.21 = f32[3,16,128]{2,1,0:T(8,128)} all-reduce(f32[3,16,128]{2,1,0:T(8,128)S(1)} %pad_maximum_fusion.4), channel_id=1, replica_groups=mesh['gz'=4,'xy'=8] {'gz','xy'}, use_global_device_ids=true, to_apply=%region_8.0 | all-reduce | flops 6144 | bytes 49152 | tf_op jit(solution)/shard_map/psum | solution.py:138
  147.2 29.7 %all-reduce.5.cloned.1.call-done = f32[3,128,128]{2,1,0:T(8,128)} async-done(((f32[3,128,128]{2,1,0:T(8,128)}), f32[3,128,128]{2,1,0:T(8,128)}) %all-reduce.5.cloned.1.call-update) | async-done | bytes 196624 | tf_op jit(solution)/shard_map/psum | solution.py:121
  176.9 1.6 copy.29
  (81 shorter events, 5.5 us)
Async XLA Ops:
  7.2 4.9 %copy-start = (f32[3,16,128]{2,1,0:T(8,128)S(1)}, f32[3,16,128]{2,1,0:T(8,128)}, u32[]{:S(2)}) copy-start(f32[3,16,128]{2,1,0:T(8,128)} %param.12) | copy-start | bytes 73732
  7.2 139.3 %all-reduce.3.cloned.1.call-start = ((), (), s32[]{:S(2)}) async-start(), calls=%async_computation | async-start | bytes 393216 | tf_op jit(solution)/shard_map/psum | solution.py:121
  7.2 13.0 %collective-permute-start = (bf16[1,1,256,128]{3,2,1,0:T(8,128)(2,1)}, bf16[1,1,256,128]{3,2,1,0:T(8,128)(2,1)S(1)}, u32[]{:S(2)}, u32[]{:S(2)}) collective-permute-start(bf16[1,1,256,128]{3,2,1,0:T(8,128)(2,1)} %param.11), channel_id=1, source_target_pairs={{0,8},{8,16},{16,24},{24,0},{1,9},{9,17},{17,25},{25,1},{2,10},{10... | collective-permute-start | bytes 196616 | tf_op jit(solution)/shard_map/ppermute | solution.py:19
  7.3 13.0 %collective-permute-start.1 = (bf16[1,1,256,128]{3,2,1,0:T(8,128)(2,1)}, bf16[1,1,256,128]{3,2,1,0:T(8,128)(2,1)S(1)}, u32[]{:S(2)}, u32[]{:S(2)}) collective-permute-start(bf16[1,1,256,128]{3,2,1,0:T(8,128)(2,1)} %param.11), channel_id=1, source_target_pairs={{8,0},{16,8},{24,16},{0,24},{9,1},{17,9},{25,17},{1,25},{10,2},{18... | collective-permute-start | bytes 196616 | tf_op jit(solution)/shard_map/ppermute | solution.py:21
  12.1 7.3 %copy-start.8 = (bf16[1,1,9,128,128]{4,3,2,1,0:T(8,128)(2,1)S(1)}, bf16[1,1,9,128,128]{4,3,2,1,0:T(8,128)(2,1)}, u32[]{:S(2)}) copy-start(bf16[1,1,9,128,128]{4,3,2,1,0:T(8,128)(2,1)} %param.7) | copy-start | bytes 884740
  12.1 8.2 %copy-start.10 = (bf16[1,1,256,128]{3,2,1,0:T(8,128)(2,1)S(1)}, bf16[1,1,256,128]{3,2,1,0:T(8,128)(2,1)}, u32[]{:S(2)}) copy-start(bf16[1,1,256,128]{3,2,1,0:T(8,128)(2,1)} %param.11) | copy-start | bytes 196612
  12.1 10.3 %copy-start.11 = (s32[1,1,32,128]{3,2,1,0:T(8,128)S(1)}, s32[1,1,32,128]{3,2,1,0:T(8,128)}, u32[]{:S(2)}) copy-start(s32[1,1,32,128]{3,2,1,0:T(8,128)} %param.9) | copy-start | bytes 49156
  20.3 11.0 %collective-permute-start.2 = (bf16[3,1,256,128]{3,2,1,0:T(8,128)(2,1)S(1)}, bf16[3,1,256,128]{3,2,1,0:T(8,128)(2,1)S(1)}, u32[]{:S(2)}, u32[]{:S(2)}) collective-permute-start(bf16[3,1,256,128]{3,2,1,0:T(8,128)(2,1)S(1)} %constant_dynamic-update-slice_fusion.9), channel_id=1, source_target_pairs={{0,1},{1,2},{2,3},{3,4},{4,5},{5,6},{6,7},{7,0},{8,9},{9,10},{10,1... | collective-permute-start | bytes 589832 | tf_op jit(solution)/shard_map/ppermute | solution.py:19
  21.9 9.4 %collective-permute-start.3 = (bf16[3,1,256,128]{3,2,1,0:T(8,128)(2,1)S(1)}, bf16[3,1,256,128]{3,2,1,0:T(8,128)(2,1)S(1)}, u32[]{:S(2)}, u32[]{:S(2)}) collective-permute-start(bf16[3,1,256,128]{3,2,1,0:T(8,128)(2,1)S(1)} %constant_dynamic-update-slice_fusion.9), channel_id=1, source_target_pairs={{1,0},{2,1},{3,2},{4,3},{5,4},{6,5},{7,6},{0,7},{9,8},{10,9},{11,1... | collective-permute-start | bytes 589832 | tf_op jit(solution)/shard_map/ppermute | solution.py:21
  48.7 2.0 %copy-start.9 = (bf16[3,128,128]{2,1,0:T(8,128)(2,1)S(1)}, bf16[3,128,128]{2,1,0:T(8,128)(2,1)}, u32[]{:S(2)}) copy-start(bf16[3,128,128]{2,1,0:T(8,128)(2,1)} %param.13) | copy-start | bytes 294916
  50.8 3.6 %copy-start.7 = (f32[1,1,9,128,128]{4,3,2,1,0:T(8,128)S(1)}, f32[1,1,9,128,128]{4,3,2,1,0:T(8,128)}, u32[]{:S(2)}) copy-start(f32[1,1,9,128,128]{4,3,2,1,0:T(8,128)} %convert_element_type.43) | copy-start | bytes 1769476
  56.5 120.4 %all-reduce.5.cloned.1.call-start = ((), (), s32[]{:S(2)}) async-start(), calls=%async_computation.1 | async-start | bytes 393216 | tf_op jit(solution)/shard_map/psum | solution.py:121
  56.6 5.4 %copy-start.5 = (f32[1,32,128,128]{3,2,0,1:T(8,128)S(1)}, f32[1,32,128,128]{3,2,0,1:T(8,128)}, u32[]{:S(2)}) copy-start(f32[1,32,128,128]{3,2,0,1:T(8,128)} %get-tuple-element.5) | copy-start | bytes 6291460
  56.6 5.4 %copy-start.6 = (f32[1,32,128,128]{3,2,0,1:T(8,128)S(1)}, f32[1,32,128,128]{3,2,0,1:T(8,128)}, u32[]{:S(2)}) copy-start(f32[1,32,128,128]{3,2,0,1:T(8,128)} %get-tuple-element.9) | copy-start | bytes 6291460
  58.7 7.0 %copy-start.1 = (f32[32,128,128]{2,1,0:T(8,128)}, f32[32,128,128]{2,1,0:T(8,128)S(1)}, u32[]{:S(2)}) copy-start(f32[32,128,128]{2,1,0:T(8,128)S(1)} %multiply_reduce_fusion.2) | copy-start | bytes 6291460
  62.0 3.8 %copy-start.3 = (f32[32,128,128]{2,1,0:T(8,128)}, f32[32,128,128]{2,1,0:T(8,128)S(1)}, u32[]{:S(2)}) copy-start(f32[32,128,128]{2,1,0:T(8,128)S(1)} %multiply_reduce_fusion) | copy-start | bytes 6291460
  88.7 1.9 %copy-start.2 = (f32[32,128,128]{2,1,0:T(8,128)S(1)}, f32[32,128,128]{2,1,0:T(8,128)}, u32[]{:S(2)}) copy-start(f32[32,128,128]{2,1,0:T(8,128)} %copy-done.1) | copy-start | bytes 6291460
  88.8 10.7 %collective-permute-start.4 = (f32[1,3,256,128]{3,2,1,0:T(8,128)S(1)}, f32[1,3,256,128]{3,2,1,0:T(8,128)S(1)}, u32[]{:S(2)}, u32[]{:S(2)}) collective-permute-start(f32[1,3,256,128]{3,2,1,0:T(8,128)S(1)} %bitcast.174), channel_id=1, source_target_pairs={{0,8},{8,16},{16,24},{24,0},{1,9},{9,17},{17,25},{25,1},{2,10},{10... | collective-permute-start | bytes 1179656 | tf_op jit(solution)/shard_map/ppermute | solution.py:19
  88.8 10.6 %collective-permute-start.5 = (f32[1,3,256,128]{3,2,1,0:T(8,128)S(1)}, f32[1,3,256,128]{3,2,1,0:T(8,128)S(1)}, u32[]{:S(2)}, u32[]{:S(2)}) collective-permute-start(f32[1,3,256,128]{3,2,1,0:T(8,128)S(1)} %bitcast.173), channel_id=1, source_target_pairs={{8,0},{16,8},{24,16},{0,24},{9,1},{17,9},{25,17},{1,25},{10,2},{18... | collective-permute-start | bytes 1179656 | tf_op jit(solution)/shard_map/ppermute | solution.py:21
  90.6 1.6 copy-start.4
  99.6 47.0 %collective-permute-start.6 = (f32[1,256,128]{2,1,0:T(8,128)S(1)}, f32[1,256,128]{2,1,0:T(8,128)S(1)}, u32[]{:S(2)}, u32[]{:S(2)}) collective-permute-start(f32[1,256,128]{2,1,0:T(8,128)S(1)} %get-tuple-element.16), channel_id=1, source_target_pairs={{0,1},{1,2},{2,3},{3,4},{4,5},{5,6},{6,7},{7,0},{8,9},{9,10},{10,1... | collective-permute-start | bytes 393224 | tf_op jit(solution)/shard_map/ppermute | solution.py:19
  102.0 44.5 %collective-permute-start.7 = (f32[1,256,128]{2,1,0:T(8,128)S(1)}, f32[1,256,128]{2,1,0:T(8,128)S(1)}, u32[]{:S(2)}, u32[]{:S(2)}) collective-permute-start(f32[1,256,128]{2,1,0:T(8,128)S(1)} %get-tuple-element.17), channel_id=1, source_target_pairs={{1,0},{2,1},{3,2},{4,3},{5,4},{6,5},{7,6},{0,7},{9,8},{10,9},{11,1... | collective-permute-start | bytes 393224 | tf_op jit(solution)/shard_map/ppermute | solution.py:21
Sparse Core Ops, SparseCore 0:
  56.7 69.5 all-reduce.2
  146.7 30.1 all-reduce.4
